TPU v7x, 128 devices: a whole 4x4x4 slice. The times are simulated.
128 devices in a mesh: layer: 4 (over y), grid: 32 (over x, z, core).
Axes of the slice: x: 4, y: 4, z: 4, core: 2. Of those that a mesh axis runs over, the one named last changes fastest.
Arguments:
- leaf_inverse: float32 [4, 32, 4, 128, 128], P('layer', 'grid'), may hold values from -1 to 2
- leaf_coupling: float32 [4, 32, 4, 128, 128], P('layer', 'grid'), may hold values from -0.5 to 0.5
- leaf_rhs: float32 [4, 32, 4, 128, 128], P('layer', 'grid'), may hold values from -6 to 6
- mid_inverse: float32 [4, 32, 2, 128, 128], P('layer', 'grid'), may hold values from -1 to 2
- mid_coupling: float32 [4, 32, 2, 128, 128], P('layer', 'grid'), may hold values from -0.375 to 0.375
- mid_rhs: float32 [4, 32, 2, 128, 128], P('layer', 'grid'), may hold values from -6 to 6
- mid_top: float32 [4, 32, 2, 4096, 128], P('layer', 'grid'), may hold values from -0.0546875 to 0.0546875
- root_inverse: float32 [4, 32, 128, 128], P('layer', 'grid'), may hold values from -1 to 2
- root_top: float32 [4, 32, 4096, 128], P('layer', 'grid'), may hold values from -0.0546875 to 0.0546875
- root_rhs: float32 [4, 32, 128, 128], P('layer', 'grid'), may hold values from -6 to 6
- top_inverse: float32 [32, 128, 128], P('grid'), may hold values from -1 to 2
- top_factor: float32 [32, 128, 4096], P('grid'), may hold values from -0.25 to 0.25
- top_rhs: float32 [32, 128, 128], P('grid'), may hold values from -6 to 6
- top_pattern: int32 [32, 32], P('grid'), may hold values from 0 to 1, as said below
Outputs:
- leaf_solution: float32 [4, 32, 4, 128, 128], P('layer', 'grid')
- mid_solution: float32 [4, 32, 2, 128, 128], P('layer', 'grid')
- root_solution: float32 [4, 32, 128, 128], P('layer', 'grid')
- top_solution: float32 [32, 128, 128], P('grid')
Inputs may be any that keep to these rules, and one draw needn't show every extreme that they name: `top_pattern`: entries (i, j) with j // 4 >= i // 4 are not read; entry (i, 0) is 1 for every i >= 4.
All inputs are finite; a program needn't handle non-finite values.
Results may differ from a plain program's by a relative error of at most 0.00011.
Values sent between devices are 32-bit elements; how exact they have to be, the bound alone decides.
No kernel may reach another device: no remote copies, remote signals or barrier semaphores. Data moves between devices by JAX's collectives and lax.ppermute only.
A program may use at most 64 MiB of HBM per device.

v0:
```python
import jax
import jax.numpy as jnp
from jax import lax
from jax.sharding import PartitionSpec as P

SPAN = 4


def product(spec, left, right):
    return jnp.einsum(
        spec, left, right, precision=lax.Precision.HIGHEST, preferred_element_type=jnp.float32
    )


def transposed(left, right):
    return lax.dot_general(
        left,
        right,
        (((0,), (0,)), ((), ())),
        precision=lax.Precision.HIGHEST,
        preferred_element_type=jnp.float32,
    )


def pack_slot(value, slot, span):
    picks = (jnp.arange(span) == slot)[:, None, None]
    return jnp.where(picks, value[None], jnp.zeros((), jnp.float32))


def local(
    leaf_inverse,
    leaf_coupling,
    leaf_rhs,
    mid_inverse,
    mid_coupling,
    mid_rhs,
    mid_top,
    root_inverse,
    root_top,
    root_rhs,
    top_inverse,
    top_factor,
    top_rhs,
    top_pattern,
):
    block_width = leaf_inverse.shape[-1]
    columns = leaf_rhs.shape[-1]
    blocks_top = lax.axis_size("grid")
    position = lax.axis_index("grid")
    span = SPAN
    group_count = blocks_top // span
    own_group = position // span
    leaf_inv = leaf_inverse[0, 0]
    leaf_links = leaf_coupling[0, 0]
    forward_leaf = product("pab,pbr->par", leaf_inv, leaf_rhs[0, 0])
    pulled = (
        product("pab,pbr->par", leaf_links, forward_leaf)
        .reshape(-1, 2, block_width, columns)
        .sum(axis=1)
    )
    forward_mid = product("mab,mbr->mar", mid_inverse[0, 0], mid_rhs[0, 0] - pulled)
    root_input = root_rhs[0, 0] - product("mab,mbr->ar", mid_coupling[0, 0], forward_mid)
    forward_root = product("ab,br->ar", root_inverse[0, 0], root_input)
    root_panel = root_top[0, 0]
    mid_panel = mid_top[0, 0]
    root_rows = root_panel
    mid_rows = mid_panel
    summed = product("kb,br->kr", root_rows, forward_root) + product(
        "mkb,mbr->kr", mid_rows, forward_mid
    )
    partial_sums = lax.psum_scatter(
        summed.reshape(1 * lax.axis_size("grid"), block_width, columns),
        "grid",
        scatter_dimension=0,
        tiled=True,
    )
    reduced = lax.psum(partial_sums, "layer")
    residual = top_rhs[0] - reduced[0]
    top_inv = top_inverse[0]
    factor_row = top_factor[0]
    pattern_row = top_pattern[0]

    def weights_of(group):
        stored = lax.dynamic_slice_in_dim(pattern_row, group * span, span)
        return jnp.where(group < own_group, stored, 0).astype(jnp.float32)

    def panel_of(group):
        return lax.dynamic_slice_in_dim(
            factor_row, group * span * block_width, span * block_width, 1
        )

    def forward_step(group, carried):
        residual, solved_own = carried
        candidate = jnp.dot(
            top_inv, residual, precision=lax.Precision.HIGHEST, preferred_element_type=jnp.float32
        )
        slot = position - group * span
        solved = lax.psum(pack_slot(candidate, slot, span), "grid")
        scaled = (weights_of(group)[:, None, None] * solved).reshape(span * block_width, columns)
        update = jnp.dot(
            panel_of(group),
            scaled,
            precision=lax.Precision.HIGHEST,
            preferred_element_type=jnp.float32,
        )
        residual = residual - update
        solved_own = jnp.where(own_group == group, candidate, solved_own)
        return (residual, solved_own)

    residual, forward_top = lax.fori_loop(
        0, group_count, forward_step, (residual, jnp.zeros_like(residual))
    )

    def contribution(group, back_own):
        terms = transposed(panel_of(group), back_own).reshape(span, block_width, columns)
        return weights_of(group)[:, None, None] * terms

    def settle(group, pulled_group, back_own):
        slot = jnp.clip(position - group * span, 0, span - 1)
        pulled_top = lax.dynamic_index_in_dim(pulled_group, slot, 0, keepdims=False)
        candidate = transposed(top_inv, forward_top - pulled_top)
        return jnp.where(own_group == group, candidate, back_own)

    def back_step(sweep_step, back_own):
        group = group_count - 1 - sweep_step
        pulled_group = lax.psum(contribution(group, back_own), "grid")
        return settle(group, pulled_group, back_own)

    back_own = lax.fori_loop(0, group_count, back_step, jnp.zeros_like(forward_top))
    shard_piece = lax.all_gather(back_own[None], "grid", axis=0, tiled=True)
    amount = shard_piece.shape[0]
    flat_rows = shard_piece.reshape(amount * block_width, columns)
    root_rows = root_panel
    mid_rows = mid_panel
    root_pull = transposed(root_rows, flat_rows)
    mid_pull = product("mkb,kr->mbr", mid_rows, flat_rows)
    back_root = product("ba,br->ar", root_inverse[0, 0], forward_root - root_pull)
    back_mid = product(
        "mba,mbr->mar",
        mid_inverse[0, 0],
        forward_mid - product("mab,ar->mbr", mid_coupling[0, 0], back_root) - mid_pull,
    )
    parent = jnp.repeat(back_mid, 2, axis=0)
    back_leaf = product(
        "pba,pbr->par", leaf_inv, forward_leaf - product("pab,par->pbr", leaf_links, parent)
    )
    return (back_leaf[None, None], back_mid[None, None], back_root[None, None], back_own[None])


def solution(mesh):
    placed = (
        P("layer", "grid", None, None, None),
        P("layer", "grid", None, None, None),
        P("layer", "grid", None, None, None),
        P("layer", "grid", None, None, None),
        P("layer", "grid", None, None, None),
        P("layer", "grid", None, None, None),
        P("layer", "grid", None, None, None),
        P("layer", "grid", None, None),
        P("layer", "grid", None, None),
        P("layer", "grid", None, None),
        P("grid", None, None),
        P("grid", None, None),
        P("grid", None, None),
        P("grid", None),
    )
    return jax.shard_map(
        local,
        mesh=mesh,
        in_specs=placed,
        out_specs=(
            P("layer", "grid", None, None, None),
            P("layer", "grid", None, None, None),
            P("layer", "grid", None, None),
            P("grid", None, None),
        ),
        check_vma=False,
    )
```

profile of v0, /device:TPU:1, one launch (start us, length us, event | category | flops | bytes accessed | tf_op | source)
XLA Modules:
  0.0 1938.6 jit_solution(1425876203916425412)
XLA Ops:
  7.2 1.1 copy.27
  8.4 1.4 fusion.43
  9.8 1.6 bitcast_reduce_fusion
  11.4 1.3 convolution_bitcast_fusion.5
  12.7 6.5 convolution_bitcast_fusion.1
  19.8 3.4 fusion.14
  23.2 2.9 copy.38
  26.2 80.7 %reduce-scatter.2.cloned.1.call-done = f32[1,128,128]{2,1,0:T(8,128)} async-done(((f32[32,128,128]{2,1,0:T(8,128)}), f32[1,128,128]{2,1,0:T(8,128)}) %reduce-scatter.2.cloned.1.call-update) | async-done | bytes 65552 | tf_op jit(solution)/shard_map/reduce_scatter | solution.py:71
  106.9 41.9 %all-reduce.4.cloned.1.call-done = f32[1,128,128]{2,1,0:T(8,128)} async-done(((f32[1,128,128]{2,1,0:T(8,128)}), f32[1,128,128]{2,1,0:T(8,128)}) %all-reduce.4.cloned.1.call-update) | async-done | bytes 65552 | tf_op jit(solution)/shard_map/psum | solution.py:77
  148.9 0.8 subtract_bitcast_fusion
  149.7 868.9 %while.34 = (s32[]{:T(128)}, f32[128,128]{1,0:T(8,128)S(1)}, f32[128,128]{1,0:T(8,128)S(1)}, f32[128,4096]{1,0:T(8,128)}, s32[]{:T(128)}, /*index=5*/s32[32]{0:T...) while((s32[]{:T(128)}, f32[128,128]{1,0:T(8,128)S(1)}, ...), condition=%wide.region_5.6_spmd.clone, body=%wide.region_3.5_spmd.clone.sunk | while | flops 126074896 | bytes 3408247 | solution.py:110
  150.9 107.7 %all-reduce.6.cloned.1.call-done = f32[4,128,128]{2,1,0:T(8,128)} async-done(((f32[4,128,128]{2,1,0:T(8,128)}), f32[4,128,128]{2,1,0:T(8,128)}) %all-reduce.6.cloned.1.call-update) | async-done | bytes 262160 | tf_op jit(solution)/shard_map/while/body/eval_jaxpr/psum | solution.py:98
  258.6 1.0 broadcast_multiply_fusion.4
  259.6 1.4 convolution_subtract_fusion.2
  262.2 104.5 %all-reduce.6.cloned.1.call-done = f32[4,128,128]{2,1,0:T(8,128)} async-done(((f32[4,128,128]{2,1,0:T(8,128)}), f32[4,128,128]{2,1,0:T(8,128)}) %all-reduce.6.cloned.1.call-update) | async-done | bytes 262160 | tf_op jit(solution)/shard_map/while/body/eval_jaxpr/psum | solution.py:98
  366.7 1.0 broadcast_multiply_fusion.4
  367.7 1.4 convolution_subtract_fusion.2
  370.3 104.5 %all-reduce.6.cloned.1.call-done = f32[4,128,128]{2,1,0:T(8,128)} async-done(((f32[4,128,128]{2,1,0:T(8,128)}), f32[4,128,128]{2,1,0:T(8,128)}) %all-reduce.6.cloned.1.call-update) | async-done | bytes 262160 | tf_op jit(solution)/shard_map/while/body/eval_jaxpr/psum | solution.py:98
  474.8 1.0 broadcast_multiply_fusion.4
  475.8 1.4 convolution_subtract_fusion.2
  478.4 104.5 %all-reduce.6.cloned.1.call-done = f32[4,128,128]{2,1,0:T(8,128)} async-done(((f32[4,128,128]{2,1,0:T(8,128)}), f32[4,128,128]{2,1,0:T(8,128)}) %all-reduce.6.cloned.1.call-update) | async-done | bytes 262160 | tf_op jit(solution)/shard_map/while/body/eval_jaxpr/psum | solution.py:98
  582.9 1.0 broadcast_multiply_fusion.4
  583.9 1.4 convolution_subtract_fusion.2
  586.5 104.8 %all-reduce.6.cloned.1.call-done = f32[4,128,128]{2,1,0:T(8,128)} async-done(((f32[4,128,128]{2,1,0:T(8,128)}), f32[4,128,128]{2,1,0:T(8,128)}) %all-reduce.6.cloned.1.call-update) | async-done | bytes 262160 | tf_op jit(solution)/shard_map/while/body/eval_jaxpr/psum | solution.py:98
  691.3 1.0 broadcast_multiply_fusion.4
  692.3 1.4 convolution_subtract_fusion.2
  694.9 104.8 %all-reduce.6.cloned.1.call-done = f32[4,128,128]{2,1,0:T(8,128)} async-done(((f32[4,128,128]{2,1,0:T(8,128)}), f32[4,128,128]{2,1,0:T(8,128)}) %all-reduce.6.cloned.1.call-update) | async-done | bytes 262160 | tf_op jit(solution)/shard_map/while/body/eval_jaxpr/psum | solution.py:98
  799.7 1.0 broadcast_multiply_fusion.4
  800.8 1.4 convolution_subtract_fusion.2
  803.3 104.8 %all-reduce.6.cloned.1.call-done = f32[4,128,128]{2,1,0:T(8,128)} async-done(((f32[4,128,128]{2,1,0:T(8,128)}), f32[4,128,128]{2,1,0:T(8,128)}) %all-reduce.6.cloned.1.call-update) | async-done | bytes 262160 | tf_op jit(solution)/shard_map/while/body/eval_jaxpr/psum | solution.py:98
  908.1 1.0 broadcast_multiply_fusion.4
  909.2 1.4 convolution_subtract_fusion.2
  911.7 104.5 %all-reduce.6.cloned.1.call-done = f32[4,128,128]{2,1,0:T(8,128)} async-done(((f32[4,128,128]{2,1,0:T(8,128)}), f32[4,128,128]{2,1,0:T(8,128)}) %all-reduce.6.cloned.1.call-update) | async-done | bytes 262160 | tf_op jit(solution)/shard_map/while/body/eval_jaxpr/psum | solution.py:98
  1016.2 1.0 broadcast_multiply_fusion.4
  1017.3 1.4 convolution_subtract_fusion.2
  1018.6 852.6 %while.35 = (s32[]{:T(128)}, f32[128,128]{0,1:T(8,128)S(1)}, s32[]{:T(128)}, s32[32]{0:T(128)S(1)}, f32[128,4096]{1,0:T(8,128)}, /*index=5*/s32[]{:T(128)}, f32[...) while((s32[]{:T(128)}, f32[128,128]{0,1:T(8,128)S(1)}, ...), condition=%wide.region_8.9_spmd.clone, body=%wide.region_6.8_spmd.clone.sunk | while | flops 126025744 | bytes 3015076 | solution.py:129
  1018.8 1.5 fusion.90
  1021.2 103.1 %all-reduce.8.cloned.1.call-done = f32[4,128,128]{2,1,0:T(8,128)} async-done(((f32[4,128,128]{2,1,0:T(8,128)}), f32[4,128,128]{2,1,0:T(8,128)}) %all-reduce.8.cloned.1.call-update) | async-done | bytes 262160 | tf_op jit(solution)/shard_map/while/body/eval_jaxpr/psum | solution.py:126
  1124.3 1.1 fusion.92
  1125.6 1.5 fusion.90
  1128.0 102.8 %all-reduce.8.cloned.1.call-done = f32[4,128,128]{2,1,0:T(8,128)} async-done(((f32[4,128,128]{2,1,0:T(8,128)}), f32[4,128,128]{2,1,0:T(8,128)}) %all-reduce.8.cloned.1.call-update) | async-done | bytes 262160 | tf_op jit(solution)/shard_map/while/body/eval_jaxpr/psum | solution.py:126
  1230.8 1.1 fusion.92
  1232.1 1.5 fusion.90
  1234.5 103.1 %all-reduce.8.cloned.1.call-done = f32[4,128,128]{2,1,0:T(8,128)} async-done(((f32[4,128,128]{2,1,0:T(8,128)}), f32[4,128,128]{2,1,0:T(8,128)}) %all-reduce.8.cloned.1.call-update) | async-done | bytes 262160 | tf_op jit(solution)/shard_map/while/body/eval_jaxpr/psum | solution.py:126
  1337.6 1.1 fusion.92
  1338.9 1.5 fusion.90
  1341.3 102.8 %all-reduce.8.cloned.1.call-done = f32[4,128,128]{2,1,0:T(8,128)} async-done(((f32[4,128,128]{2,1,0:T(8,128)}), f32[4,128,128]{2,1,0:T(8,128)}) %all-reduce.8.cloned.1.call-update) | async-done | bytes 262160 | tf_op jit(solution)/shard_map/while/body/eval_jaxpr/psum | solution.py:126
  1444.1 1.1 fusion.92
  1445.4 1.5 fusion.90
  1447.8 102.8 %all-reduce.8.cloned.1.call-done = f32[4,128,128]{2,1,0:T(8,128)} async-done(((f32[4,128,128]{2,1,0:T(8,128)}), f32[4,128,128]{2,1,0:T(8,128)}) %all-reduce.8.cloned.1.call-update) | async-done | bytes 262160 | tf_op jit(solution)/shard_map/while/body/eval_jaxpr/psum | solution.py:126
  1550.6 1.1 fusion.92
  1551.9 1.5 fusion.90
  1554.3 102.8 %all-reduce.8.cloned.1.call-done = f32[4,128,128]{2,1,0:T(8,128)} async-done(((f32[4,128,128]{2,1,0:T(8,128)}), f32[4,128,128]{2,1,0:T(8,128)}) %all-reduce.8.cloned.1.call-update) | async-done | bytes 262160 | tf_op jit(solution)/shard_map/while/body/eval_jaxpr/psum | solution.py:126
  1657.1 1.1 fusion.92
  1658.4 1.5 fusion.90
  1660.8 102.8 %all-reduce.8.cloned.1.call-done = f32[4,128,128]{2,1,0:T(8,128)} async-done(((f32[4,128,128]{2,1,0:T(8,128)}), f32[4,128,128]{2,1,0:T(8,128)}) %all-reduce.8.cloned.1.call-update) | async-done | bytes 262160 | tf_op jit(solution)/shard_map/while/body/eval_jaxpr/psum | solution.py:126
  1763.6 1.1 fusion.92
  1764.9 1.5 fusion.90
  1767.3 102.8 %all-reduce.8.cloned.1.call-done = f32[4,128,128]{2,1,0:T(8,128)} async-done(((f32[4,128,128]{2,1,0:T(8,128)}), f32[4,128,128]{2,1,0:T(8,128)}) %all-reduce.8.cloned.1.call-update) | async-done | bytes 262160 | tf_op jit(solution)/shard_map/while/body/eval_jaxpr/psum | solution.py:126
  1870.1 1.1 fusion.92
  1872.0 1.6 copy.32
  1873.6 46.3 %all-gather.3.cloned.1.call-done = f32[4096,128]{0,1:T(8,128)} async-done(((f32[128,128]{0,1:T(8,128)}), f32[4096,128]{0,1:T(8,128)}) %all-gather.3.cloned.1.call-update) | async-done | bytes 2097168 | tf_op jit(solution)/shard_map/all_gather | solution.py:130
  1919.9 3.9 fusion.34
  1924.3 3.8 fusion.28
  (124 shorter events, 22.4 us)
Async XLA Ops:
  7.2 12.7 copy-start
  7.2 99.7 %reduce-scatter.2.cloned.1.call-start = ((), (), s32[]{:S(2)}) async-start(), calls=%async_computation.1 | async-start | bytes 2162688 | tf_op jit(solution)/shard_map/reduce_scatter | solution.py:71
  12.7 6.6 copy-start.6
  12.7 6.6 copy-start.10
  12.7 6.8 copy-start.8
  26.1 122.7 %copy-start.9 = (f32[1,128,128]{2,1,0:T(8,128)S(1)}, f32[1,128,128]{2,1,0:T(8,128)}, u32[]{:S(2)}) copy-start(f32[1,128,128]{2,1,0:T(8,128)} %param.30) | copy-start | bytes 196612
  26.1 123.6 %copy-start.3 = (f32[1,128,128]{2,1,0:T(8,128)S(1)}, f32[1,128,128]{2,1,0:T(8,128)}, u32[]{:S(2)}) copy-start(f32[1,128,128]{2,1,0:T(8,128)} %param.28) | copy-start | bytes 196612
  26.1 123.6 %copy-start.11 = (s32[1,32]{1,0:T(1,128)S(1)}, s32[1,32]{1,0:T(1,128)}, u32[]{:S(2)}) copy-start(s32[1,32]{1,0:T(1,128)} %param.31) | copy-start | bytes 388
  26.2 122.7 %all-reduce.4.cloned.1.call-start = ((), (), s32[]{:S(2)}) async-start(), calls=%async_computation.2 | async-start | bytes 131072 | tf_op jit(solution)/shard_map/psum | solution.py:77
  149.7 108.9 %all-reduce.6.cloned.1.call-start = ((), (), s32[]{:S(2)}) async-start(), calls=%async_computation.4 | async-start | bytes 524288 | tf_op jit(solution)/shard_map/while/body/eval_jaxpr/psum | solution.py:98
  261.0 105.7 %all-reduce.6.cloned.1.call-start = ((), (), s32[]{:S(2)}) async-start(), calls=%async_computation.4 | async-start | bytes 524288 | tf_op jit(solution)/shard_map/while/body/eval_jaxpr/psum | solution.py:98
  369.1 105.7 %all-reduce.6.cloned.1.call-start = ((), (), s32[]{:S(2)}) async-start(), calls=%async_computation.4 | async-start | bytes 524288 | tf_op jit(solution)/shard_map/while/body/eval_jaxpr/psum | solution.py:98
  477.2 105.7 %all-reduce.6.cloned.1.call-start = ((), (), s32[]{:S(2)}) async-start(), calls=%async_computation.4 | async-start | bytes 524288 | tf_op jit(solution)/shard_map/while/body/eval_jaxpr/psum | solution.py:98
  585.3 106.0 %all-reduce.6.cloned.1.call-start = ((), (), s32[]{:S(2)}) async-start(), calls=%async_computation.4 | async-start | bytes 524288 | tf_op jit(solution)/shard_map/while/body/eval_jaxpr/psum | solution.py:98
  693.7 106.0 %all-reduce.6.cloned.1.call-start = ((), (), s32[]{:S(2)}) async-start(), calls=%async_computation.4 | async-start | bytes 524288 | tf_op jit(solution)/shard_map/while/body/eval_jaxpr/psum | solution.py:98
  802.1 106.0 %all-reduce.6.cloned.1.call-start = ((), (), s32[]{:S(2)}) async-start(), calls=%async_computation.4 | async-start | bytes 524288 | tf_op jit(solution)/shard_map/while/body/eval_jaxpr/psum | solution.py:98
  910.5 105.7 %all-reduce.6.cloned.1.call-start = ((), (), s32[]{:S(2)}) async-start(), calls=%async_computation.4 | async-start | bytes 524288 | tf_op jit(solution)/shard_map/while/body/eval_jaxpr/psum | solution.py:98
  1018.6 105.7 %all-reduce.8.cloned.1.call-start = ((), (), s32[]{:S(2)}) async-start(), calls=%async_computation.5 | async-start | bytes 524288 | tf_op jit(solution)/shard_map/while/body/eval_jaxpr/psum | solution.py:126
  1125.5 105.4 %all-reduce.8.cloned.1.call-start = ((), (), s32[]{:S(2)}) async-start(), calls=%async_computation.5 | async-start | bytes 524288 | tf_op jit(solution)/shard_map/while/body/eval_jaxpr/psum | solution.py:126
  1232.0 105.7 %all-reduce.8.cloned.1.call-start = ((), (), s32[]{:S(2)}) async-start(), calls=%async_computation.5 | async-start | bytes 524288 | tf_op jit(solution)/shard_map/while/body/eval_jaxpr/psum | solution.py:126
  1338.8 105.3 %all-reduce.8.cloned.1.call-start = ((), (), s32[]{:S(2)}) async-start(), calls=%async_computation.5 | async-start | bytes 524288 | tf_op jit(solution)/shard_map/while/body/eval_jaxpr/psum | solution.py:126
  1445.3 105.4 %all-reduce.8.cloned.1.call-start = ((), (), s32[]{:S(2)}) async-start(), calls=%async_computation.5 | async-start | bytes 524288 | tf_op jit(solution)/shard_map/while/body/eval_jaxpr/psum | solution.py:126
  1551.8 105.3 %all-reduce.8.cloned.1.call-start = ((), (), s32[]{:S(2)}) async-start(), calls=%async_computation.5 | async-start | bytes 524288 | tf_op jit(solution)/shard_map/while/body/eval_jaxpr/psum | solution.py:126
  1658.3 105.4 %all-reduce.8.cloned.1.call-start = ((), (), s32[]{:S(2)}) async-start(), calls=%async_computation.5 | async-start | bytes 524288 | tf_op jit(solution)/shard_map/while/body/eval_jaxpr/psum | solution.py:126
  1764.8 105.3 %all-reduce.8.cloned.1.call-start = ((), (), s32[]{:S(2)}) async-start(), calls=%async_computation.5 | async-start | bytes 524288 | tf_op jit(solution)/shard_map/while/body/eval_jaxpr/psum | solution.py:126
  1871.3 0.6 copy-start.2
  1871.3 48.7 %all-gather.3.cloned.1.call-start = ((), (), s32[]{:S(2)}) async-start(), calls=%async_computation.3 | async-start | bytes 2162688 | tf_op jit(solution)/shard_map/all_gather | solution.py:130
  1919.9 4.4 copy-start.1
  1924.3 3.8 copy-start.7
  1924.3 4.2 copy-start.5
  1928.1 1.0 copy-start.4
Sparse Core Ops, SparseCore 0:
  26.3 80.5 reduce-scatter.1
  109.2 39.6 all-reduce.3
  154.7 103.8 all-reduce.5
  265.7 100.9 all-reduce.5
  373.8 100.9 all-reduce.5
  481.9 100.9 all-reduce.5
  590.3 100.9 all-reduce.5
  698.7 100.9 all-reduce.5
  807.1 100.9 all-reduce.5
  915.2 100.9 all-reduce.5
  1023.3 100.9 all-reduce.7
  1129.8 100.9 all-reduce.7
  1236.6 100.9 all-reduce.7
  1343.1 100.9 all-reduce.7
  1449.6 100.9 all-reduce.7
  1556.1 100.9 all-reduce.7
  1662.6 100.9 all-reduce.7
  1769.1 100.9 all-reduce.7
  1875.1 44.7 all-gather.2
where the time goes:
time: 1940 us
  waiting for transfers between devices  1830 us (94%)
  matrix products  58.2 us (3%)
  other arithmetic  23.1 us (1%)
    psum x8, waiting for transfers between devices, forward_step(): solved = lax.psum(pack_slot(candidate, slot, span), 'grid')  840 us
    psum x8, waiting for transfers between devices, back_step(): pulled_group = lax.psum(contribution(group, back_own), 'grid')  823 us
    reduce_scatter x1, waiting for transfers between devices, local(): lax.psum_scatter(summed.reshape(1 * lax.axis_size('grid'), block_width, c...  80.7 us
    all_gather x1, waiting for transfers between devices, local(): shard_piece = lax.all_gather(back_own[None], 'grid', axis=0, tiled=True)  46.3 us
    psum x1, waiting for transfers between devices, local(): reduced = lax.psum(partial_sums, 'layer')  41.9 us
  transfers between devices with their start and end apart: 19, of which 19 were waited for; matrix products, arithmetic and copies ran while one was open for 0% of the time, Pallas kernels for 0%

commit v1 on v0

--- a/solution.py
+++ b/solution.py
@@ -123,7 +123,7 @@
 
     def back_step(sweep_step, back_own):
         group = group_count - 1 - sweep_step
-        pulled_group = lax.psum(contribution(group, back_own), "grid")
+        pulled_group = jnp.sum(lax.all_gather(contribution(group, back_own), "grid"), axis=0)
         return settle(group, pulled_group, back_own)
 
     back_own = lax.fori_loop(0, group_count, back_step, jnp.zeros_like(forward_top))

time: 1940 us -> 1570 us (0.81)
  waiting for transfers between devices: 1830 us -> 1440 us
  other arithmetic: 23.1 us -> 53.7 us
    psum x8 -> x0, waiting for transfers between devices: 823 us -> none  [back_step(): pulled_group = lax.psum(contribution(group, back_own), 'grid')]
    all_gather x0 -> x8, waiting for transfers between devices: none -> 428 us  [back_step(): lax.all_gather(contribution(group, back_own), 'grid')]
    reduce_sum x0 -> x8, other arithmetic: none -> 30.6 us  [back_step(): jnp.sum(lax.all_gather(contribution(group, back_own), 'grid'), axis=0)]
where the time goes in v1:
time: 1570 us
  waiting for transfers between devices  1440 us (92%)
  other arithmetic  53.7 us (3%)
  matrix products  51.5 us (3%)
    psum x8, waiting for transfers between devices, forward_step(): solved = lax.psum(pack_slot(candidate, slot, span), 'grid')  840 us
    all_gather x8, waiting for transfers between devices, back_step(): lax.all_gather(contribution(group, back_own), 'grid')  428 us
    reduce_scatter x1, waiting for transfers between devices, local(): lax.psum_scatter(summed.reshape(1 * lax.axis_size('grid'), block_width, c...  80.7 us
    all_gather x1, waiting for transfers between devices, local(): shard_piece = lax.all_gather(back_own[None], 'grid', axis=0, tiled=True)  45.9 us
    psum x1, waiting for transfers between devices, local(): reduced = lax.psum(partial_sums, 'layer')  41.9 us
  transfers between devices with their start and end apart: 19, of which 19 were waited for; matrix products, arithmetic and copies ran while one was open for 0% of the time, Pallas kernels for 0%

profile of v1, /device:TPU:1, one launch (start us, length us, event | category | flops | bytes accessed | tf_op | source)
XLA Modules:
  0.0 1567.1 jit_solution(1560871684191804267)
XLA Ops:
  7.2 1.1 copy.27
  8.4 1.4 fusion.43
  9.8 1.6 bitcast_reduce_fusion
  11.4 1.3 convolution_bitcast_fusion.5
  12.7 6.5 convolution_bitcast_fusion.1
  19.8 3.4 fusion.14
  23.2 2.9 copy.38
  26.2 80.7 %reduce-scatter.2.cloned.1.call-done = f32[1,128,128]{2,1,0:T(8,128)} async-done(((f32[32,128,128]{2,1,0:T(8,128)}), f32[1,128,128]{2,1,0:T(8,128)}) %reduce-scatter.2.cloned.1.call-update) | async-done | bytes 65552 | tf_op jit(solution)/shard_map/reduce_scatter | solution.py:71
  107.0 41.9 %all-reduce.3.cloned.1.call-done = f32[1,128,128]{2,1,0:T(8,128)} async-done(((f32[1,128,128]{2,1,0:T(8,128)}), f32[1,128,128]{2,1,0:T(8,128)}) %all-reduce.3.cloned.1.call-update) | async-done | bytes 65552 | tf_op jit(solution)/shard_map/psum | solution.py:77
  148.9 0.8 subtract_bitcast_fusion
  149.8 868.9 %while.34 = (s32[]{:T(128)}, f32[128,128]{1,0:T(8,128)S(1)}, f32[128,128]{1,0:T(8,128)S(1)}, f32[128,4096]{1,0:T(8,128)}, s32[]{:T(128)}, /*index=5*/s32[32]{0:T...) while((s32[]{:T(128)}, f32[128,128]{1,0:T(8,128)S(1)}, ...), condition=%wide.region_5.6_spmd.clone, body=%wide.region_3.5_spmd.clone.sunk | while | flops 126074896 | bytes 3408255 | solution.py:110
  151.0 107.7 %all-reduce.5.cloned.1.call-done = f32[4,128,128]{2,1,0:T(8,128)} async-done(((f32[4,128,128]{2,1,0:T(8,128)}), f32[4,128,128]{2,1,0:T(8,128)}) %all-reduce.5.cloned.1.call-update) | async-done | bytes 262160 | tf_op jit(solution)/shard_map/while/body/eval_jaxpr/psum | solution.py:98
  258.6 1.0 broadcast_multiply_fusion.4
  259.7 1.4 convolution_subtract_fusion.2
  262.3 104.5 %all-reduce.5.cloned.1.call-done = f32[4,128,128]{2,1,0:T(8,128)} async-done(((f32[4,128,128]{2,1,0:T(8,128)}), f32[4,128,128]{2,1,0:T(8,128)}) %all-reduce.5.cloned.1.call-update) | async-done | bytes 262160 | tf_op jit(solution)/shard_map/while/body/eval_jaxpr/psum | solution.py:98
  366.7 1.0 broadcast_multiply_fusion.4
  367.8 1.4 convolution_subtract_fusion.2
  370.3 104.5 %all-reduce.5.cloned.1.call-done = f32[4,128,128]{2,1,0:T(8,128)} async-done(((f32[4,128,128]{2,1,0:T(8,128)}), f32[4,128,128]{2,1,0:T(8,128)}) %all-reduce.5.cloned.1.call-update) | async-done | bytes 262160 | tf_op jit(solution)/shard_map/while/body/eval_jaxpr/psum | solution.py:98
  474.8 1.0 broadcast_multiply_fusion.4
  475.9 1.4 convolution_subtract_fusion.2
  478.4 104.5 %all-reduce.5.cloned.1.call-done = f32[4,128,128]{2,1,0:T(8,128)} async-done(((f32[4,128,128]{2,1,0:T(8,128)}), f32[4,128,128]{2,1,0:T(8,128)}) %all-reduce.5.cloned.1.call-update) | async-done | bytes 262160 | tf_op jit(solution)/shard_map/while/body/eval_jaxpr/psum | solution.py:98
  582.9 1.0 broadcast_multiply_fusion.4
  584.0 1.4 convolution_subtract_fusion.2
  586.5 104.8 %all-reduce.5.cloned.1.call-done = f32[4,128,128]{2,1,0:T(8,128)} async-done(((f32[4,128,128]{2,1,0:T(8,128)}), f32[4,128,128]{2,1,0:T(8,128)}) %all-reduce.5.cloned.1.call-update) | async-done | bytes 262160 | tf_op jit(solution)/shard_map/while/body/eval_jaxpr/psum | solution.py:98
  691.3 1.0 broadcast_multiply_fusion.4
  692.4 1.4 convolution_subtract_fusion.2
  695.0 104.8 %all-reduce.5.cloned.1.call-done = f32[4,128,128]{2,1,0:T(8,128)} async-done(((f32[4,128,128]{2,1,0:T(8,128)}), f32[4,128,128]{2,1,0:T(8,128)}) %all-reduce.5.cloned.1.call-update) | async-done | bytes 262160 | tf_op jit(solution)/shard_map/while/body/eval_jaxpr/psum | solution.py:98
  799.7 1.0 broadcast_multiply_fusion.4
  800.8 1.4 convolution_subtract_fusion.2
  803.4 104.8 %all-reduce.5.cloned.1.call-done = f32[4,128,128]{2,1,0:T(8,128)} async-done(((f32[4,128,128]{2,1,0:T(8,128)}), f32[4,128,128]{2,1,0:T(8,128)}) %all-reduce.5.cloned.1.call-update) | async-done | bytes 262160 | tf_op jit(solution)/shard_map/while/body/eval_jaxpr/psum | solution.py:98
  908.1 1.0 broadcast_multiply_fusion.4
  909.2 1.4 convolution_subtract_fusion.2
  911.8 104.5 %all-reduce.5.cloned.1.call-done = f32[4,128,128]{2,1,0:T(8,128)} async-done(((f32[4,128,128]{2,1,0:T(8,128)}), f32[4,128,128]{2,1,0:T(8,128)}) %all-reduce.5.cloned.1.call-update) | async-done | bytes 262160 | tf_op jit(solution)/shard_map/while/body/eval_jaxpr/psum | solution.py:98
  1016.2 1.0 broadcast_multiply_fusion.4
  1017.3 1.4 convolution_subtract_fusion.2
  1018.7 481.6 %while.35 = (s32[]{:T(128)}, f32[128,128]{0,1:T(8,128)S(1)}, s32[]{:T(128)}, s32[32]{0:T(128)S(1)}, f32[128,4096]{1,0:T(8,128)}, /*index=5*/s32[]{:T(128)}, f32[...) while((s32[]{:T(128)}, f32[128,128]{0,1:T(8,128)S(1)}, ...), condition=%wide.region_8.9_spmd.clone, body=%wide.region_6.8_spmd.clone.sunk | while | flops 127991824 | bytes 36045232 | solution.py:129
  1018.8 1.5 fusion.90
  1021.2 54.1 %all-gather.6.cloned.1.call-done = f32[32,4,128,128]{3,2,1,0:T(8,128)} async-done(((f32[1,4,128,128]{3,2,1,0:T(8,128)}), f32[32,4,128,128]{3,2,1,0:T(8,128)}) %all-gather.6.cloned.1.call-update) | async-done | bytes 8388624 | tf_op jit(solution)/shard_map/while/body/eval_jaxpr/all_gather | solution.py:126
  1075.3 3.8 reduce_sum.29
  1079.6 1.5 fusion.90
  1082.0 53.4 %all-gather.6.cloned.1.call-done = f32[32,4,128,128]{3,2,1,0:T(8,128)} async-done(((f32[1,4,128,128]{3,2,1,0:T(8,128)}), f32[32,4,128,128]{3,2,1,0:T(8,128)}) %all-gather.6.cloned.1.call-update) | async-done | bytes 8388624 | tf_op jit(solution)/shard_map/while/body/eval_jaxpr/all_gather | solution.py:126
  1135.4 3.8 reduce_sum.29
  1139.7 1.5 fusion.90
  1142.1 53.7 %all-gather.6.cloned.1.call-done = f32[32,4,128,128]{3,2,1,0:T(8,128)} async-done(((f32[1,4,128,128]{3,2,1,0:T(8,128)}), f32[32,4,128,128]{3,2,1,0:T(8,128)}) %all-gather.6.cloned.1.call-update) | async-done | bytes 8388624 | tf_op jit(solution)/shard_map/while/body/eval_jaxpr/all_gather | solution.py:126
  1195.8 3.8 reduce_sum.29
  1200.1 1.5 fusion.90
  1202.4 53.4 %all-gather.6.cloned.1.call-done = f32[32,4,128,128]{3,2,1,0:T(8,128)} async-done(((f32[1,4,128,128]{3,2,1,0:T(8,128)}), f32[32,4,128,128]{3,2,1,0:T(8,128)}) %all-gather.6.cloned.1.call-update) | async-done | bytes 8388624 | tf_op jit(solution)/shard_map/while/body/eval_jaxpr/all_gather | solution.py:126
  1255.8 3.8 reduce_sum.29
  1260.1 1.5 fusion.90
  1262.5 53.4 %all-gather.6.cloned.1.call-done = f32[32,4,128,128]{3,2,1,0:T(8,128)} async-done(((f32[1,4,128,128]{3,2,1,0:T(8,128)}), f32[32,4,128,128]{3,2,1,0:T(8,128)}) %all-gather.6.cloned.1.call-update) | async-done | bytes 8388624 | tf_op jit(solution)/shard_map/while/body/eval_jaxpr/all_gather | solution.py:126
  1315.9 3.8 reduce_sum.29
  1320.2 1.5 fusion.90
  1322.6 53.4 %all-gather.6.cloned.1.call-done = f32[32,4,128,128]{3,2,1,0:T(8,128)} async-done(((f32[1,4,128,128]{3,2,1,0:T(8,128)}), f32[32,4,128,128]{3,2,1,0:T(8,128)}) %all-gather.6.cloned.1.call-update) | async-done | bytes 8388624 | tf_op jit(solution)/shard_map/while/body/eval_jaxpr/all_gather | solution.py:126
  1376.0 3.8 reduce_sum.29
  1380.2 1.5 fusion.90
  1382.6 53.4 %all-gather.6.cloned.1.call-done = f32[32,4,128,128]{3,2,1,0:T(8,128)} async-done(((f32[1,4,128,128]{3,2,1,0:T(8,128)}), f32[32,4,128,128]{3,2,1,0:T(8,128)}) %all-gather.6.cloned.1.call-update) | async-done | bytes 8388624 | tf_op jit(solution)/shard_map/while/body/eval_jaxpr/all_gather | solution.py:126
  1436.0 3.8 reduce_sum.29
  1440.3 1.5 fusion.90
  1442.7 53.4 %all-gather.6.cloned.1.call-done = f32[32,4,128,128]{3,2,1,0:T(8,128)} async-done(((f32[1,4,128,128]{3,2,1,0:T(8,128)}), f32[32,4,128,128]{3,2,1,0:T(8,128)}) %all-gather.6.cloned.1.call-update) | async-done | bytes 8388624 | tf_op jit(solution)/shard_map/while/body/eval_jaxpr/all_gather | solution.py:126
  1496.1 3.8 reduce_sum.29
  1501.0 1.6 copy.32
  1502.5 45.9 %all-gather.4.cloned.1.call-done = f32[4096,128]{0,1:T(8,128)} async-done(((f32[128,128]{0,1:T(8,128)}), f32[4096,128]{0,1:T(8,128)}) %all-gather.4.cloned.1.call-update) | async-done | bytes 2097168 | tf_op jit(solution)/shard_map/all_gather | solution.py:130
  1548.5 3.9 fusion.34
  1552.9 3.8 fusion.28
  (132 shorter events, 24.8 us)
Async XLA Ops:
  7.2 12.7 copy-start
  7.2 99.7 %reduce-scatter.2.cloned.1.call-start = ((), (), s32[]{:S(2)}) async-start(), calls=%async_computation.1 | async-start | bytes 2162688 | tf_op jit(solution)/shard_map/reduce_scatter | solution.py:71
  12.7 6.6 copy-start.6
  12.7 6.6 copy-start.10
  12.7 6.9 copy-start.8
  26.1 122.8 %copy-start.9 = (f32[1,128,128]{2,1,0:T(8,128)S(1)}, f32[1,128,128]{2,1,0:T(8,128)}, u32[]{:S(2)}) copy-start(f32[1,128,128]{2,1,0:T(8,128)} %param.30) | copy-start | bytes 196612
  26.1 123.6 %copy-start.3 = (f32[1,128,128]{2,1,0:T(8,128)S(1)}, f32[1,128,128]{2,1,0:T(8,128)}, u32[]{:S(2)}) copy-start(f32[1,128,128]{2,1,0:T(8,128)} %param.28) | copy-start | bytes 196612
  26.1 123.6 %copy-start.11 = (s32[1,32]{1,0:T(1,128)S(1)}, s32[1,32]{1,0:T(1,128)}, u32[]{:S(2)}) copy-start(s32[1,32]{1,0:T(1,128)} %param.31) | copy-start | bytes 388
  26.2 122.7 %all-reduce.3.cloned.1.call-start = ((), (), s32[]{:S(2)}) async-start(), calls=%async_computation.2 | async-start | bytes 131072 | tf_op jit(solution)/shard_map/psum | solution.py:77
  149.8 108.9 %all-reduce.5.cloned.1.call-start = ((), (), s32[]{:S(2)}) async-start(), calls=%async_computation.4 | async-start | bytes 524288 | tf_op jit(solution)/shard_map/while/body/eval_jaxpr/psum | solution.py:98
  261.0 105.7 %all-reduce.5.cloned.1.call-start = ((), (), s32[]{:S(2)}) async-start(), calls=%async_computation.4 | async-start | bytes 524288 | tf_op jit(solution)/shard_map/while/body/eval_jaxpr/psum | solution.py:98
  369.1 105.7 %all-reduce.5.cloned.1.call-start = ((), (), s32[]{:S(2)}) async-start(), calls=%async_computation.4 | async-start | bytes 524288 | tf_op jit(solution)/shard_map/while/body/eval_jaxpr/psum | solution.py:98
  477.2 105.7 %all-reduce.5.cloned.1.call-start = ((), (), s32[]{:S(2)}) async-start(), calls=%async_computation.4 | async-start | bytes 524288 | tf_op jit(solution)/shard_map/while/body/eval_jaxpr/psum | solution.py:98
  585.3 106.0 %all-reduce.5.cloned.1.call-start = ((), (), s32[]{:S(2)}) async-start(), calls=%async_computation.4 | async-start | bytes 524288 | tf_op jit(solution)/shard_map/while/body/eval_jaxpr/psum | solution.py:98
  693.7 106.0 %all-reduce.5.cloned.1.call-start = ((), (), s32[]{:S(2)}) async-start(), calls=%async_computation.4 | async-start | bytes 524288 | tf_op jit(solution)/shard_map/while/body/eval_jaxpr/psum | solution.py:98
  802.2 106.0 %all-reduce.5.cloned.1.call-start = ((), (), s32[]{:S(2)}) async-start(), calls=%async_computation.4 | async-start | bytes 524288 | tf_op jit(solution)/shard_map/while/body/eval_jaxpr/psum | solution.py:98
  910.6 105.7 %all-reduce.5.cloned.1.call-start = ((), (), s32[]{:S(2)}) async-start(), calls=%async_computation.4 | async-start | bytes 524288 | tf_op jit(solution)/shard_map/while/body/eval_jaxpr/psum | solution.py:98
  1018.7 56.7 %all-gather.6.cloned.1.call-start = ((), (), s32[]{:S(2)}) async-start(), calls=%async_computation.5 | async-start | bytes 8650752 | tf_op jit(solution)/shard_map/while/body/eval_jaxpr/all_gather | solution.py:126
  1079.5 55.9 %all-gather.6.cloned.1.call-start = ((), (), s32[]{:S(2)}) async-start(), calls=%async_computation.5 | async-start | bytes 8650752 | tf_op jit(solution)/shard_map/while/body/eval_jaxpr/all_gather | solution.py:126
  1139.5 56.2 %all-gather.6.cloned.1.call-start = ((), (), s32[]{:S(2)}) async-start(), calls=%async_computation.5 | async-start | bytes 8650752 | tf_op jit(solution)/shard_map/while/body/eval_jaxpr/all_gather | solution.py:126
  1199.9 55.9 %all-gather.6.cloned.1.call-start = ((), (), s32[]{:S(2)}) async-start(), calls=%async_computation.5 | async-start | bytes 8650752 | tf_op jit(solution)/shard_map/while/body/eval_jaxpr/all_gather | solution.py:126
  1260.0 55.9 %all-gather.6.cloned.1.call-start = ((), (), s32[]{:S(2)}) async-start(), calls=%async_computation.5 | async-start | bytes 8650752 | tf_op jit(solution)/shard_map/while/body/eval_jaxpr/all_gather | solution.py:126
  1320.0 55.9 %all-gather.6.cloned.1.call-start = ((), (), s32[]{:S(2)}) async-start(), calls=%async_computation.5 | async-start | bytes 8650752 | tf_op jit(solution)/shard_map/while/body/eval_jaxpr/all_gather | solution.py:126
  1380.1 55.9 %all-gather.6.cloned.1.call-start = ((), (), s32[]{:S(2)}) async-start(), calls=%async_computation.5 | async-start | bytes 8650752 | tf_op jit(solution)/shard_map/while/body/eval_jaxpr/all_gather | solution.py:126
  1440.2 55.9 %all-gather.6.cloned.1.call-start = ((), (), s32[]{:S(2)}) async-start(), calls=%async_computation.5 | async-start | bytes 8650752 | tf_op jit(solution)/shard_map/while/body/eval_jaxpr/all_gather | solution.py:126
  1500.2 0.6 copy-start.2
  1500.2 48.2 %all-gather.4.cloned.1.call-start = ((), (), s32[]{:S(2)}) async-start(), calls=%async_computation.3 | async-start | bytes 2162688 | tf_op jit(solution)/shard_map/all_gather | solution.py:130
  1548.5 4.4 copy-start.1
  1552.8 3.8 copy-start.7
  1552.9 4.9 copy-start.5
  1556.6 1.8 copy-start.4
Sparse Core Ops, SparseCore 0:
  26.3 80.5 reduce-scatter.1
  109.2 39.6 all-reduce.2
  154.7 103.8 all-reduce.4
  265.7 100.9 all-reduce.4
  373.8 100.9 all-reduce.4
  481.9 100.9 all-reduce.4
  590.3 100.9 all-reduce.4
  698.7 100.9 all-reduce.4
  807.1 100.9 all-reduce.4
  915.2 100.9 all-reduce.4
  1022.3 52.9 all-gather.5
  1082.8 52.5 all-gather.5
  1143.2 52.5 all-gather.5
  1203.3 52.5 all-gather.5
  1263.3 52.5 all-gather.5
  1323.4 52.5 all-gather.5
  1383.5 52.5 all-gather.5
  1443.5 52.5 all-gather.5
  1504.1 44.3 all-gather.3
